TPU v7x, 256 devices: a whole 4x4x8 slice. The times are simulated.
256 devices in a mesh: occ: 4 (over y), vir: 32 (over z, x), pair: 2 (over core).
Axes of the slice: x: 4, y: 4, z: 8, core: 2. Of those that a mesh axis runs over, the one named last changes fastest.
Arguments:
- amplitudes: bfloat16 [2, 4096, 8192], P('pair', 'occ', 'vir'), may hold values from -6 to 6
- hh_integrals: bfloat16 [2, 4096, 4096], P('pair', 'occ'), may hold values from -0.09375 to 0.09375
- ladder_blocks: bfloat16 [32, 64, 128, 128], P('vir'), may hold values from -0.09375 to 0.09375
- block_target: int32 [32, 64], P('vir'), may hold values from 0 to 63, each once within a row
- block_live: int32 [32, 64], P('vir'), may hold values from 0 to 1
Outputs:
- residual: bfloat16 [2, 4096, 8192], P('pair', 'occ', 'vir')
Inputs may be any that keep to these rules, and one draw needn't show every extreme that they name: `block_target`: each row is a permutation: the 64 blocks of one index of vir reach every tile exactly once.
All inputs are finite; a program needn't handle non-finite values.
Results may differ from a plain program's by a relative error of at most 0.0037.
Values may be sent and summed in bfloat16 or wider, within the bound.
A program may use at most 128 MiB of HBM per device.

v0:
```python
import jax
import jax.numpy as jnp
from jax import lax
from jax.sharding import PartitionSpec as P

TILE = 128


def partner(block, axis, stride):
    count = lax.axis_size(axis)
    route = []
    for low in range(count):
        high = low | 1 << stride
        if high != low and high < count:
            route += [(low, high), (high, low)]
    return lax.ppermute(block, axis, route)


def on_device(amplitudes, hh_integrals, ladder_blocks, block_target, block_live):
    vir_count = lax.axis_size("vir")
    ladder_input = amplitudes[0]
    row_count = ladder_input.shape[0]
    col_span = ladder_input.shape[1]
    tile_count = col_span // TILE
    block_count = tile_count * vir_count
    live_mask = block_live[0].astype(jnp.bfloat16)
    masked_blocks = ladder_blocks[0] * live_mask[:, None, None]
    inverse = (
        jnp.zeros((block_count,), jnp.int32)
        .at[block_target[0]]
        .set(jnp.arange(block_count, dtype=jnp.int32))
    )
    tile_view = ladder_input.reshape(row_count, tile_count, TILE)
    grouped = masked_blocks.reshape(tile_count, vir_count, TILE, TILE)
    partials = jnp.einsum(
        "pyc,ykcd->ykpd", tile_view, grouped, preferred_element_type=jnp.float32
    ).astype(jnp.bfloat16)
    partials = partials.reshape(block_count, row_count, TILE)[inverse]
    partials = partials.reshape(vir_count, tile_count, row_count, TILE)
    arrived = lax.all_to_all(partials, "vir", split_axis=0, concat_axis=0, tiled=True)
    ladder = jnp.sum(arrived, axis=0, dtype=jnp.float32)
    ladder_flat = ladder.transpose(1, 0, 2).reshape(row_count, col_span)
    weights = hh_integrals[0]
    hole_term = jnp.dot(
        weights,
        lax.all_gather(amplitudes, "occ", axis=1, tiled=True)[0],
        preferred_element_type=jnp.float32,
    )
    unsymmetric = hole_term + ladder_flat
    mirrored = partner(unsymmetric, "pair", 0)
    return (unsymmetric + mirrored).astype(jnp.bfloat16)[None]


def solution(mesh):
    return jax.shard_map(
        on_device,
        mesh=mesh,
        in_specs=(
            P("pair", "occ", "vir"),
            P("pair", "occ", None),
            P("vir", None, None, None),
            P("vir", None),
            P("vir", None),
        ),
        out_specs=P("pair", "occ", "vir"),
        check_vma=False,
    )
```

profile of v0, /device:TPU:5, one launch (start us, length us, event | category | flops | bytes accessed | tf_op | source)
XLA Modules:
  0.0 470.4 jit_solution(8787770331255220508)
XLA Ops:
  6.5 3.1 copy.8
  9.7 1.2 reshape_squeeze.3
  10.9 0.7 convert_reduce_fusion.1
  11.5 0.1 convert_element_type.23
  11.6 0.7 fusion.12
  12.3 0.8 scatter_custom_fusion
  13.1 8.1 %convolution_convert_fusion = bf16[2,32,128,1024]{3,2,1,0:T(8,128)(2,1)} fusion(bf16[2,32,128,128]{2,3,1,0:T(8,128)(2,1)S(1)} %copy.8, bf16[2,32]{1,0:T(2,128)(2,1)S(1)} %convert_element_type.23, bf16[1024,2,128,1]{2,1,0,3:T(2,128)(2,1)S(1)} %bitcast.28), kind=kOutput, calls=%fused_computation.3 | convolution fusion | flops 2156920832 | bytes 19398784 | tf_op jit(solution)/shard_map/pyc,ykcd->ykpd/dot_general | solution.py:35
  21.2 13.4 %gather_fusion = bf16[64,1024,128]{1,2,0:T(8,128)(2,1)} fusion(bf16[64,1024,128]{1,2,0:T(8,128)(2,1)} %bitcast.26, s32[1024]{0:T(1024)S(1)} %pad_clamp_fusion), kind=kCustom, calls=%fused_computation | custom fusion | bytes 33554688 | tf_op jit(solution)/shard_map/gather | solution.py:38
  34.6 11.1 %all-to-all-start = ((bf16[32,2,1024,128]{2,3,1,0:T(8,128)(2,1)}), bf16[32,2,1024,128]{2,3,1,0:T(8,128)(2,1)}, u32[]{:S(2)}, u32[]{:S(2)}) async-start(bf16[32,2,1024,128]{2,3,1,0:T(8,128)(2,1)} %bitcast.25), calls=%async_computation | async-start | bytes 33554432 | tf_op jit(solution)/shard_map/all_to_all | solution.py:40
  45.6 0.0 all-gather.2.cloned.1.call-start
  45.7 0.7 all-gather.2.cloned.1.call-update
  46.4 398.8 %all-to-all-done = bf16[32,2,1024,128]{2,3,1,0:T(8,128)(2,1)} async-done(((bf16[32,2,1024,128]{2,3,1,0:T(8,128)(2,1)}), bf16[32,2,1024,128]{2,3,1,0:T(8,128)(2,1)}, u32[]{:S(2)}, u32[]{:S(2)}) %all-to-all-start) | async-done | bytes 16777248 | tf_op jit(solution)/shard_map/all_to_all | solution.py:40
  445.2 7.0 %convert_reduce_fusion = f32[2,1024,128]{1,2,0:T(8,128)S(1)} fusion(bf16[32,2,1024,128]{2,3,1,0:T(8,128)(2,1)} %all-to-all-done), kind=kLoop, calls=%fused_computation.2 | loop fusion | flops 16515072 | bytes 17825792 | tf_op jit(solution)/shard_map/reduce_sum | solution.py:41
  452.2 0.3 copy.14
  452.5 0.0 all-gather.2.cloned.1.call-done
  452.6 6.3 %fusion.4 = f32[1024,256]{1,0:T(8,128)S(1)} fusion(f32[1024,256]{1,0:T(8,128)S(1)} %copy.14, bf16[1,4096,256]{2,1,0:T(8,128)(2,1)} %all-gather.2.cloned.1.call-done, bf16[1,1024,4096]{2,1,0:T(8,128)(2,1)} %param.6), kind=kOutput, calls=%fused_computation.8 | convolution fusion | flops 2147745792 | bytes 12582912 | tf_op jit(solution)/shard_map/dot_general | solution.py:44
  458.9 1.5 collective-permute-start
  460.4 2.3 collective-permute-done
  462.7 0.9 fusion.10
  (3 shorter events, 0.0 us)
Async XLA Ops:
  34.6 410.7 %all-to-all-start = ((bf16[32,2,1024,128]{2,3,1,0:T(8,128)(2,1)}), bf16[32,2,1024,128]{2,3,1,0:T(8,128)(2,1)}, u32[]{:S(2)}, u32[]{:S(2)}) async-start(bf16[32,2,1024,128]{2,3,1,0:T(8,128)(2,1)} %bitcast.25), calls=%async_computation | async-start | bytes 33554432 | tf_op jit(solution)/shard_map/all_to_all | solution.py:40
  45.6 406.9 %all-gather.2.cloned.1.call-start = ((), (), s32[]{:S(2)}) async-start(), calls=%async_computation.1 | async-start | bytes 2621440 | tf_op jit(solution)/shard_map/all_gather | solution.py:46
  458.9 3.8 collective-permute-start
Sparse Core Ops, SparseCore 0:
  48.3 35.0 all-gather.1
where the time goes:
time: 471 us; the launch traced here: 470 us
  waiting for transfers between devices  402 us (85%)
  local copies, waits for them, and re-layouts  18.9 us (4%)
  matrix products  14.4 us (3%)
  between operations  13.5 us (3%)
  starting transfers between devices  12.6 us (3%)
  other arithmetic  9.24 us (2%)
    all_to_all x1, waiting for transfers between devices, on_device(): lax.all_to_all(partials, 'vir', split_axis=0, concat_axis=0, tiled=True)  399 us
    gather x1, local copies, waits for them, and re-layouts, on_device(): partials = partials.reshape(block_count, row_count, TILE)[inverse]  13.4 us
    all_to_all x1, starting transfers between devices, on_device(): lax.all_to_all(partials, 'vir', split_axis=0, concat_axis=0, tiled=True)  11.1 us
  transfers between devices with their start and end apart: 3, of which 2 were waited for; matrix products, arithmetic and copies ran while one was open for 2% of the time, Pallas kernels for 0%

commit v1 on v0

v1 whole, which is shorter than its diff:
```python
import jax
import jax.numpy as jnp
from jax import lax
from jax.experimental import pallas as pl
from jax.experimental.pallas import tpu as pltpu
from jax.sharding import PartitionSpec as P

MESH = pl.DeviceIdType.MESH
TILE = 128
NX = 4
NY = 4
NZ = 8
NT = 64
ROWS = 1024
HALF = 512
COLS = 256
CH = 128
NC = HALF // CH
F32 = jnp.float32
BF16 = jnp.bfloat16


def kernel(inv, live, amp, hh, blocks, out,
           amp_v, aoth, s_all, a_all, h_v, l_raw, l_own, l_in, meta_own, meta_in,
           l_dense, zs, zr, acc, hx, fin, ofin,
           sem_lraw, sem_amp, sem_h, pa_s, pa_r, ya_s, ya_r, xs_s, xs_r, xl_s, xl_r,
           xm_s, xm_r, pl_s, pl_r, z_s, z_r, ph_s, ph_r, po_s, po_r, lo_s):
    y = lax.axis_index("occ")
    v = lax.axis_index("vir")
    p = lax.axis_index("pair")
    z = v // NX
    x = v % NX

    def at_x(dx):
        return {"occ": y, "vir": z * NX + (x + dx) % NX, "pair": p}

    def at_y(dy):
        return {"occ": (y + dy) % NY, "vir": v, "pair": p}

    def at_z(dz):
        return {"occ": y, "vir": ((z + dz) % NZ) * NX + x, "pair": p}

    mate = {"occ": y, "vir": v, "pair": 1 - p}

    def remote(src, dst, ss, rs, dev):
        return pltpu.make_async_remote_copy(
            src_ref=src, dst_ref=dst, send_sem=ss, recv_sem=rs,
            device_id=dev, device_id_type=MESH)

    def crow(c):
        return pl.ds(pl.multiple_of(c * CH, CH), CH)

    get_lraw = pltpu.make_async_copy(blocks.at[0], l_raw, sem_lraw)
    get_amp = pltpu.make_async_copy(amp.at[0], amp_v, sem_amp)
    get_h = [
        pltpu.make_async_copy(
            hh.at[0, :, pl.ds(pl.multiple_of(((y + k) % NY) * ROWS, ROWS), ROWS)],
            h_v.at[k], sem_h.at[k])
        for k in range(NY)
    ]
    get_lraw.start()
    get_amp.start()
    for g in get_h:
        g.start()

    barrier = pltpu.get_barrier_semaphore()
    peers = [at_x(1), at_x(2), at_x(3), at_y(1), at_y(2), at_y(3), at_z(1), at_z(NZ - 1), mate]
    for dev in peers:
        pl.semaphore_signal(barrier, inc=1, device_id=dev, device_id_type=MESH)

    get_lraw.wait()

    def sort_block(i, carry):
        d = i // 8
        t = (i // 4) % 2
        dx = i % 4
        tile = 2 * (((z + d) % NZ) * NX + (x + dx) % NX) + t
        r = inv[tile]
        l_own[d, t, dx] = l_raw[r]
        alive = live[r].astype(F32)
        upper = jnp.where(r < NT // 2, alive, 0.0)
        row = d * 4 + t * 2
        meta_own[dx, pl.ds(row, 1), :] = jnp.full((1, TILE), upper, F32)
        meta_own[dx, pl.ds(row + 1, 1), :] = jnp.full((1, TILE), alive - upper, F32)
        return carry

    lax.fori_loop(0, NT, sort_block, 0)
    pl.semaphore_wait(barrier, len(peers))

    def pair_amp(c):
        return remote(
            amp.at[0, pl.ds(pl.multiple_of((1 - p) * HALF + c * CH, CH), CH)],
            aoth.at[crow(c)], pa_s.at[c], pa_r.at[c], mate)

    def y_amp(dy):
        return remote(amp.at[0], a_all.at[NY - dy - 1], ya_s.at[dy - 1], ya_r.at[NY - dy - 1], at_y(dy))

    def x_meta(dx):
        return remote(meta_own.at[dx], meta_in.at[NX - dx - 1], xm_s.at[dx - 1], xm_r.at[NX - dx - 1], at_x(dx))

    def x_block(d, dx):
        return remote(l_own.at[d, p, dx], l_in.at[d, p, NX - dx - 1],
                      xl_s.at[d, dx - 1], xl_r.at[d, NX - dx - 1], at_x(dx))

    def x_sum(c, dx):
        return remote(s_all.at[0, crow(c)], s_all.at[NX - dx, crow(c)],
                      xs_s.at[c, dx - 1], xs_r.at[c, NX - dx - 1], at_x(dx))

    def pair_block(d):
        return remote(l_in.at[d, p], l_in.at[d, p], pl_s.at[d], pl_r.at[d], mate)

    ORDER = (1, 3, 2)
    for c in range(NC):
        pair_amp(c).start()
    for dx in ORDER:
        x_meta(dx).start()
        x_block(4, dx).start()
    for dy in ORDER:
        y_amp(dy).start()
    get_amp.wait()

    def send_sum(c):
        pair_amp(c).wait_recv()
        mine = amp_v[pl.ds(pl.multiple_of(p * HALF + c * CH, CH), CH), :]
        s_all[0, crow(c), :] = (mine.astype(F32) + aoth[crow(c), :].astype(F32)).astype(BF16)
        for dx in ORDER:
            x_sum(c, dx).start()

    def send_blocks(*ds):
        for d in ds:
            for dx in ORDER:
                x_block(d, dx).start()

    send_sum(0)
    send_sum(1)
    send_blocks(3, 5)
    send_sum(2)
    send_sum(3)
    send_blocks(2, 6, 1, 7, 0)

    def hole(k, a_ref, first):
        def step(i, carry):
            rows = pl.ds(pl.multiple_of(i * 256, 256), 256)
            term = jnp.dot(h_v[k, rows, :], a_ref[...], preferred_element_type=F32)
            if first:
                acc[rows, :] = term
            else:
                acc[rows, :] += term
            return carry
        lax.fori_loop(0, ROWS // 256, step, 0)

    def gather_blocks(*ds):
        for d in ds:
            for dx in ORDER:
                x_block(d, dx).wait_recv()
            pair_block(d).start()
        for d in ds:
            pltpu.make_async_remote_copy(
                src_ref=l_in.at[d, 1 - p], dst_ref=l_in.at[d, 1 - p], send_sem=pl_s.at[d],
                recv_sem=pl_r.at[d], device_id=mate, device_id_type=MESH).wait_recv()
            for k in range(NX):
                for t in range(2):
                    row = d * 4 + t * 2
                    if k == 0:
                        block = l_own[d, t, 0]
                        m0 = meta_own[0, row:row + 1, :]
                        m1 = meta_own[0, row + 1:row + 2, :]
                    else:
                        block = l_in[d, t, k - 1]
                        m0 = meta_in[k - 1, row:row + 1, :]
                        m1 = meta_in[k - 1, row + 1:row + 2, :]
                    cols = slice(t * TILE, (t + 1) * TILE)
                    l_dense[d, k * 256:k * 256 + 128, cols] = block * m0.astype(BF16)
                    l_dense[d, k * 256 + 128:k * 256 + 256, cols] = block * m1.astype(BF16)

    def product(c, d):
        total = jnp.dot(s_all[0, crow(c), :], l_dense[d, 0:256, :], preferred_element_type=F32)
        for k in range(1, NX):
            total += jnp.dot(s_all[k, crow(c), :], l_dense[d, k * 256:(k + 1) * 256, :],
                             preferred_element_type=F32)
        return total

    def z_rows(h, c):
        size = CH // 2 if h == 0 else CH
        return pl.ds(pl.multiple_of(c * size, size), size)

    def z_copy(way, h, c):
        rows = z_rows(h, c)
        return remote(zs.at[way, h, rows], zr.at[way, h, rows], z_s.at[way, h, c], z_r.at[way, h, c],
                      at_z(1 if way == 0 else NZ - 1))

    def z_step(h, c):
        if h == 0:
            for dx in ORDER:
                x_sum(c, dx).wait_recv()
            total = product(c, 4)
            for way in range(2):
                zs[way, 0, z_rows(0, c), :] = total[way * 64:(way + 1) * 64].astype(BF16)
                z_copy(way, 0, c).start()
            return
        for way in range(2):
            total = product(c, 4 - h if way == 0 else 4 + h)
            z_copy(way, h - 1, c).wait_recv()
            got = zr[way, h - 1, z_rows(h - 1, c), :].astype(F32)
            if h == 1:
                lo = pl.ds(pl.multiple_of(c * CH, CH), 64)
                hi = pl.ds(pl.multiple_of(c * CH + 64, 64), 64)
                if way == 0:
                    zs[way, h, lo, :] = (total[:64] + got).astype(BF16)
                    zs[way, h, hi, :] = total[64:].astype(BF16)
                else:
                    zs[way, h, lo, :] = total[:64].astype(BF16)
                    zs[way, h, hi, :] = (total[64:] + got).astype(BF16)
            else:
                zs[way, h, crow(c), :] = (total + got).astype(BF16)
            z_copy(way, h, c).start()

    def z_steps(lo, hi, *hs):
        def step(c, carry):
            for h in hs:
                z_step(h, c)
            return carry
        lax.fori_loop(lo, hi, step, 0)

    get_h[0].wait()
    hole(0, amp_v, True)
    for dx in ORDER:
        x_meta(dx).wait_recv()
    gather_blocks(4)
    z_steps(0, 2, 0)
    gather_blocks(3, 5)
    z_steps(0, 2, 1)
    z_steps(2, 4, 0, 1)
    for k in (1, 3):
        get_h[k].wait()
        y_amp(NY - k).wait_recv()
        hole(k, a_all.at[k - 1], False)
    gather_blocks(2, 6)
    z_steps(0, 4, 2)
    gather_blocks(1, 7)
    z_steps(0, 4, 3)
    get_h[2].wait()
    y_amp(2).wait_recv()
    hole(2, a_all.at[1], False)
    pair_hole = remote(
        acc.at[pl.ds(pl.multiple_of((1 - p) * HALF, HALF), HALF)], hx, ph_s, ph_r, mate)
    pair_hole.start()
    gather_blocks(0)

    def own_product(c, carry):
        fin[crow(c), :] = product(c, 0)
        return carry

    lax.fori_loop(0, NC, own_product, 0)
    pair_hole.wait_recv()

    def out_copies(c):
        rows = pl.ds(pl.multiple_of(p * HALF + c * CH, CH), CH)
        return (
            pltpu.make_async_copy(ofin.at[crow(c)], out.at[0, rows], lo_s.at[c]),
            remote(ofin.at[crow(c)], out.at[0, rows], po_s.at[c], po_r.at[c], mate),
        )

    def finish(c, carry):
        z_copy(0, 3, c).wait_recv()
        z_copy(1, 3, c).wait_recv()
        rows = pl.ds(pl.multiple_of(p * HALF + c * CH, CH), CH)
        total = fin[crow(c), :] + acc[rows, :] + hx[crow(c), :]
        total += zr[0, 3, crow(c), :].astype(F32) + zr[1, 3, crow(c), :].astype(F32)
        ofin[crow(c), :] = total.astype(BF16)
        for copy in out_copies(c):
            copy.start()
        return carry

    lax.fori_loop(0, NC, finish, 0)

    pair_hole.wait_send()
    for dx in ORDER:
        x_meta(dx).wait_send()
        y_amp(dx).wait_send()

    def drain_d(d, carry):
        for dx in ORDER:
            x_block(d, dx).wait_send()
        pair_block(d).wait_send()
        return carry

    lax.fori_loop(0, NZ, drain_d, 0)

    def drain_c(c, carry):
        pair_amp(c).wait_send()
        for dx in ORDER:
            x_sum(c, dx).wait_send()
        for way in range(2):
            for h in range(4):
                z_copy(way, h, c).wait_send()
        keep, give = out_copies(c)
        keep.wait()
        give.wait()
        return carry

    lax.fori_loop(0, NC, drain_c, 0)


def on_device(amplitudes, hh_integrals, ladder_blocks, block_target, block_live):
    index = jnp.arange(NT, dtype=jnp.int32)
    hit = block_target[0][None, :] == index[:, None]
    inverse = jnp.sum(jnp.where(hit, index[None, :], 0), axis=1)
    dma = pltpu.SemaphoreType.DMA
    any_space = pl.BlockSpec(memory_space=pl.ANY)
    smem = pl.BlockSpec(memory_space=pltpu.SMEM)
    return pl.pallas_call(
        kernel,
        out_shape=jax.ShapeDtypeStruct((1, ROWS, COLS), BF16),
        in_specs=[smem, smem, any_space, any_space, any_space],
        out_specs=any_space,
        scratch_shapes=[
            pltpu.VMEM((ROWS, COLS), BF16),
            pltpu.VMEM((HALF, COLS), BF16),
            pltpu.VMEM((NX, HALF, COLS), BF16),
            pltpu.VMEM((NY - 1, ROWS, COLS), BF16),
            pltpu.VMEM((NY, ROWS, ROWS), BF16),
            pltpu.VMEM((NT, TILE, TILE), BF16),
            pltpu.VMEM((NZ, 2, NX, TILE, TILE), BF16),
            pltpu.VMEM((NZ, 2, NX - 1, TILE, TILE), BF16),
            pltpu.VMEM((NX, 4 * NZ, TILE), F32),
            pltpu.VMEM((NX - 1, 4 * NZ, TILE), F32),
            pltpu.VMEM((NZ, NX * COLS, COLS), BF16),
            pltpu.VMEM((2, 4, HALF, COLS), BF16),
            pltpu.VMEM((2, 4, HALF, COLS), BF16),
            pltpu.VMEM((ROWS, COLS), F32),
            pltpu.VMEM((HALF, COLS), F32),
            pltpu.VMEM((HALF, COLS), F32),
            pltpu.VMEM((HALF, COLS), BF16),
            dma, dma, dma((NY,)),
            dma((NC,)), dma((NC,)),
            dma((NY - 1,)), dma((NY - 1,)),
            dma((NC, NX - 1)), dma((NC, NX - 1)),
            dma((NZ, NX - 1)), dma((NZ, NX - 1)),
            dma((NX - 1,)), dma((NX - 1,)),
            dma((NZ,)), dma((NZ,)),
            dma((2, 4, NC)), dma((2, 4, NC)),
            dma, dma,
            dma((NC,)), dma((NC,)),
            dma((NC,)),
        ],
        compiler_params=pltpu.CompilerParams(
            collective_id=0, has_side_effects=True, vmem_limit_bytes=56 * 2**20),
        cost_estimate=pl.CostEstimate(
            flops=4 * ROWS * 4096 * COLS, bytes_accessed=12 * 2**20, transcendentals=0),
        name="ladder_hole",
    )(inverse, block_live[0], amplitudes, hh_integrals, ladder_blocks)


def solution(mesh):
    return jax.shard_map(
        on_device,
        mesh=mesh,
        in_specs=(
            P("pair", "occ", "vir"),
            P("pair", "occ", None),
            P("vir", None, None, None),
            P("vir", None),
            P("vir", None),
        ),
        out_specs=P("pair", "occ", "vir"),
        check_vma=False,
    )
```

time: 471 us -> 62.6 us (0.13)
  the two profiles are of different devices: /device:TPU:5 before, /device:TPU:1 now
where the time goes in v1:
time: 62.6 us; the launch traced here: 62.4 us
  Pallas kernels  59.3 us (95%)
  local copies, waits for them, and re-layouts  1.87 us (3%)
  other arithmetic  1.28 us (2%)
    pallas_call x1, Pallas kernels, on_device(): pl.pallas_call(kernel, out_shape=jax.ShapeDtypeStruct((1, ROWS, COLS), BF...  59.3 us
    unnamed x1, local copies, waits for them, and re-layouts  1.87 us
    reduce_sum x1, other arithmetic, on_device(): inverse = jnp.sum(jnp.where(hit, index[None, :], 0), axis=1)  1.28 us

profile of v1, /device:TPU:1, one launch (start us, length us, event | category | flops | bytes accessed | tf_op | source)
XLA Modules:
  0.0 62.4 jit_solution(14767530127283891594)
XLA Ops:
  0.0 1.3 %select_reduce_fusion.inv = s32[64]{0:T(128)} fusion(s32[64]{0:T(128)} %bitcast.2), kind=kLoop, calls=%fused_computation | loop fusion | flops 12224 | bytes 512 | tf_op jit(solution)/shard_map/reduce_sum | solution.py:308
  1.3 59.3 %ladder_hole.1 = bf16[1,1024,256]{2,1,0:T(8,128)(2,1)} custom-call(s32[64]{0:T(128)} %select_reduce_fusion.inv, s32[64]{0:T(128)} %bitcast.3, bf16[1,1024,256]{2,1,0:T(8,128)(2,1)} %amp.1, bf16[1,1024,4096]{2,1,0:T(8,128)(2,1)} %hh.1, bf16[1,64,128,128]{3,2,1,0:T(8,128)(2,1)} %blocks.1), custom_call_target="tpu_custom_call" | custom-call | flops 4294967296 | bytes 12582912 | tf_op jit(solution)/shard_map/ladder_hole/pallas_call | solution.py:312
  60.5 1.9 %copy.7 = bf16[1,1024,256]{2,1,0:T(8,128)(2,1)} copy(bf16[1,1024,256]{2,1,0:T(8,128)(2,1)} %ladder_hole.1) | data formatting | bytes 1048576

commit v2 on v1

v2 whole, which is shorter than its diff:
```python
import jax
import jax.numpy as jnp
from jax import lax
from jax.experimental import pallas as pl
from jax.experimental.pallas import tpu as pltpu
from jax.sharding import PartitionSpec as P

MESH = pl.DeviceIdType.MESH
TILE = 128
NX = 4
NY = 4
NZ = 8
NT = 64
ROWS = 1024
HALF = 512
COLS = 256
CH = 128
NC = HALF // CH
NP = 4
PIECE = ROWS // NP
DIRECT = (4,)
SHARED = (3, 5)

PLAN = (
    ("LX", 3), ("LX", 5), ("LS", 4), ("SS", 1), ("LY", 5), ("SS", 3), ("LY", 3), ("SS", 0), ("META",),
    ("LZ", 5), ("LZ", 3), ("LP", 4), ("SH", 1), ("YS", 1), ("SH", 3), ("LS", 6), ("LP", 3), ("SH", 0),
    ("SS", 2), ("LB", 4), ("LS", 2), ("Z", 0, 3), ("LP", 5), ("LS", 0), ("YS", 3), ("LH", 6), ("Z", 0, 0),
    ("Z", 0, 1), ("SH", 2), ("LB", 3), ("LB", 5), ("Z", 1, 3), ("YS", 2), ("LH", 2), ("YS", 0), ("LS", 7),
    ("Z", 1, 0), ("LH", 0), ("LP", 6), ("YP", 1), ("LS", 1), ("Z", 0, 2), ("LP", 2), ("Z", 1, 1), ("LH", 7),
    ("LP", 0), ("LB", 6), ("LB", 2), ("Z", 2, 3), ("LH", 1), ("Z", 1, 2), ("YP", 3), ("Z", 2, 0), ("LP", 7),
    ("HO", 0), ("YP", 0), ("Z", 2, 1), ("LP", 1), ("HO", 2), ("LB", 0), ("OP",), ("YP", 2), ("Z", 2, 2),
    ("LB", 7), ("HO", 1), ("LB", 1), ("Z", 3, 0), ("Z", 3, 3), ("Z", 3, 2), ("HO", 3), ("Z", 3, 1), ("PH",),
    ("FIN", 2), ("FIN", 3), ("FIN", 0), ("FIN", 1),
)
F32 = jnp.float32
BF16 = jnp.bfloat16


def kernel(target, live, amp, hh, blocks, out,
           amp_v, aoth, s_all, a_all, h_v, l_raw, l_own, l_in, l_via, meta_own, meta_in, target_v, live_v, code_v, code,
           l_dense, zs, zr, acc, hx, fin,
           sem_target, sem_live, sem_lraw, sem_amp, sem_code, sem_h, pa_s, pa_r, ya_s, ya_r, xs_s, xs_r, xl_s, xl_r, yl_s, yl_r,
           xm_s, xm_r, pl_s, pl_r, z_s, z_r, ph_s, ph_r, po_s, po_r):
    y = lax.axis_index("occ")
    v = lax.axis_index("vir")
    p = lax.axis_index("pair")
    z = v // NX
    x = v % NX
    far = 1 + 2 * p

    def at_x(dx):
        return {"occ": y, "vir": z * NX + (x + dx) % NX, "pair": p}

    def at_y(dy):
        return {"occ": (y + dy) % NY, "vir": v, "pair": p}

    def at_z(dz):
        return {"occ": y, "vir": ((z + dz) % NZ) * NX + x, "pair": p}

    mate = {"occ": y, "vir": v, "pair": 1 - p}

    def remote(src, dst, ss, rs, dev):
        return pltpu.make_async_remote_copy(
            src_ref=src, dst_ref=dst, send_sem=ss, recv_sem=rs,
            device_id=dev, device_id_type=MESH)

    def crow(c):
        return pl.ds(pl.multiple_of(c * CH, CH), CH)

    barrier = pltpu.get_barrier_semaphore()
    peers = [at_x(1), at_x(2), at_x(3), at_y(1), at_y(3), at_z(1), at_z(NZ - 1), mate]
    for dev in peers:
        pl.semaphore_signal(barrier, inc=1, device_id=dev, device_id_type=MESH)

    get_lraw = pltpu.make_async_copy(blocks.at[0], l_raw, sem_lraw)
    get_amp = pltpu.make_async_copy(amp.at[0], amp_v, sem_amp)
    get_h = [
        pltpu.make_async_copy(
            hh.at[0, :, pl.ds(pl.multiple_of(((y + k) % NY) * ROWS, ROWS), ROWS)],
            h_v.at[k], sem_h.at[k])
        for k in range(NY)
    ]
    get_target = pltpu.make_async_copy(target, target_v, sem_target)
    get_live = pltpu.make_async_copy(live, live_v, sem_live)
    get_target.start()
    get_live.start()
    get_lraw.start()
    get_amp.start()
    get_target.wait()
    get_live.wait()

    entry = lax.broadcasted_iota(jnp.int32, (NT, NT), 1)
    hit = jnp.broadcast_to(target_v[...], (NT, NT)) == lax.broadcasted_iota(jnp.int32, (NT, NT), 0)
    value = 2 * entry + jnp.broadcast_to(live_v[...], (NT, NT))
    found = jnp.max(jnp.where(hit, value, 0), axis=1, keepdims=True)
    code_v[...] = jnp.broadcast_to(found, (NT, TILE))
    get_code = pltpu.make_async_copy(code_v, code, sem_code)
    get_code.start()

    def sort_blocks(*ds):
        for d in ds:
            for t in range(2):
                for dx in range(NX):
                    tile = 2 * (((z + d) % NZ) * NX + (x + dx) % NX) + t
                    l_own[d, t, dx] = l_raw[code[tile, 0] // 2]

    def sort_meta(i, carry):
        d = i // 8
        t = (i // 4) % 2
        dx = i % 4
        tile = 2 * (((z + d) % NZ) * NX + (x + dx) % NX) + t
        both = code[tile, 0]
        alive = (both % 2).astype(F32)
        upper = jnp.where(both < NT, alive, 0.0)
        row = d * 4 + t * 2
        meta_own[dx, pl.ds(row, 1), :] = jnp.full((1, TILE), upper, F32)
        meta_own[dx, pl.ds(row + 1, 1), :] = jnp.full((1, TILE), alive - upper, F32)
        return carry

    pl.semaphore_wait(barrier, len(peers))

    def pair_amp(c):
        return remote(
            amp.at[0, pl.ds(pl.multiple_of((1 - p) * HALF + c * CH, CH), CH)],
            aoth.at[crow(c)], pa_s.at[c], pa_r.at[c], mate)

    def y_amp(j, i):
        rows = pl.ds(j * PIECE, PIECE)
        return remote(amp.at[0, rows], a_all.at[2 - 2 * i, rows], ya_s.at[j, i], ya_r.at[j, i], at_y(1 + 2 * i))

    def y_hop(j):
        rows = pl.ds(j * PIECE, PIECE)
        return remote(a_all.at[2 - 2 * p, rows], a_all.at[1, rows], ya_s.at[j, 2], ya_r.at[j, 2], at_y(far))

    def x_meta(i):
        return remote(meta_own.at[1 + 2 * i], meta_in.at[2 - 2 * i], xm_s.at[i], xm_r.at[i], at_x(1 + 2 * i))

    def x_meta_two():
        return remote(meta_own.at[2], meta_in.at[1], xm_s.at[2], xm_r.at[2], at_x(2))

    def x_block(d, i):
        return remote(l_own.at[d, p, 1 + 2 * i], l_in.at[d, p, 2 - 2 * i],
                      xl_s.at[d, i], xl_r.at[d, i], at_x(1 + 2 * i))

    def x_via(d):
        return remote(l_own.at[d, p, 2], l_via.at[d], xl_s.at[d, 2], xl_r.at[d, 2], at_x(far))

    def x_two(d):
        return remote(l_own.at[d, p, 2], l_in.at[d, p, 1], xl_s.at[d, 3], xl_r.at[d, 3], at_x(2))

    def x_hop(d):
        if d in DIRECT:
            return x_two(d)
        return remote(l_via.at[d], l_in.at[d, p, 1], xl_s.at[d, 3], xl_r.at[d, 3], at_x(far))

    def x_sum(c, i):
        return remote(s_all.at[0, crow(c)], s_all.at[3 - 2 * i, crow(c)],
                      xs_s.at[c, i], xs_r.at[c, i], at_x(1 + 2 * i))

    def x_sum_hop(c):
        return remote(s_all.at[3 - 2 * p, crow(c)], s_all.at[2, crow(c)],
                      xs_s.at[c, 2], xs_r.at[c, 2], at_x(far))

    def pair_block(d):
        return remote(l_in.at[d, p], l_in.at[d, p], pl_s.at[d], pl_r.at[d], mate)

    def send_blocks(*ds):
        for d in ds:
            if d in DIRECT:
                x_two(d).start()
            else:
                x_via(d).start()
            x_block(d, 0).start()
            x_block(d, 1).start()

    def hop_blocks(*ds):
        for d in ds:
            x_via(d).wait_recv()
            x_hop(d).start()

    def send_sum(c):
        pair_amp(c).wait_recv()
        mine = amp_v[pl.ds(pl.multiple_of(p * HALF + c * CH, CH), CH), :]
        s_all[0, crow(c), :] = (mine.astype(F32) + aoth[crow(c), :].astype(F32)).astype(BF16)
        x_sum(c, 0).start()
        x_sum(c, 1).start()

    def hop_sum(c):
        x_sum(c, p).wait_recv()
        x_sum_hop(c).start()

    def hole(k, a_ref, first):
        def step(i, carry):
            rows = pl.ds(pl.multiple_of(i * 256, 256), 256)
            term = jnp.dot(h_v[k, rows, :], a_ref[...], preferred_element_type=F32)
            if first:
                acc[rows, :] = term
            else:
                acc[rows, :] += term
            return carry
        lax.fori_loop(0, ROWS // 256, step, 0)

    def quarter(q):
        return pl.ds(pl.multiple_of((q % NY) * 32, 32), 32)

    def x_share(d, dx):
        return remote(l_own.at[d, p, dx, quarter(y)], l_in.at[d, p, NX - dx - 1, quarter(y)],
                      xl_s.at[d, dx - 1], xl_r.at[d, NX - dx - 1], at_x(dx))

    def y_share(d, i):
        return remote(l_in.at[d, p, :, quarter(y)], l_in.at[d, p, :, quarter(y)],
                      yl_s.at[d, i], yl_r.at[d, i], at_y(1 + 2 * i))

    def y_share_in(d, i):
        part = l_in.at[d, p, :, quarter(y + 3 - 2 * i)]
        return remote(part, part, yl_s.at[d, i], yl_r.at[d, i], at_y(1 + 2 * i))

    def y_share_hop(d):
        part = l_in.at[d, p, :, quarter(y + 3 - 2 * p)]
        return remote(part, part, yl_s.at[d, 2], yl_r.at[d, 2], at_y(far))

    def y_share_last(d):
        part = l_in.at[d, p, :, quarter(y + 2)]
        return remote(part, part, yl_s.at[d, 2], yl_r.at[d, 2], at_y(far))

    def share_x(d):
        get_code_once()
        sort_blocks(d)
        for dx in (2, 1, 3):
            x_share(d, dx).start()

    def share_y(d):
        for dx in (1, 3, 2):
            x_share(d, dx).wait_recv()
        y_share(d, 0).start()
        y_share(d, 1).start()

    def share_pass(d):
        y_share_in(d, p).wait_recv()
        y_share_hop(d).start()

    def swap_blocks(*ds):
        for d in ds:
            if d in SHARED:
                y_share_in(d, 1 - p).wait_recv()
                y_share_last(d).wait_recv()
            else:
                x_block(d, 0).wait_recv()
                x_block(d, 1).wait_recv()
                x_hop(d).wait_recv()
            pair_block(d).start()

    def build_blocks(*ds):
        for d in ds:
            pltpu.make_async_remote_copy(
                src_ref=l_in.at[d, 1 - p], dst_ref=l_in.at[d, 1 - p], send_sem=pl_s.at[d],
                recv_sem=pl_r.at[d], device_id=mate, device_id_type=MESH).wait_recv()
            for k in range(NX):
                for t in range(2):
                    row = d * 4 + t * 2
                    if k == 0:
                        block = l_own[d, t, 0]
                        m0 = meta_own[0, row:row + 1, :]
                        m1 = meta_own[0, row + 1:row + 2, :]
                    else:
                        block = l_in[d, t, k - 1]
                        m0 = meta_in[k - 1, row:row + 1, :]
                        m1 = meta_in[k - 1, row + 1:row + 2, :]
                    cols = slice(t * TILE, (t + 1) * TILE)
                    l_dense[d, k * 256:k * 256 + 128, cols] = block * m0.astype(BF16)
                    l_dense[d, k * 256 + 128:k * 256 + 256, cols] = block * m1.astype(BF16)

    def product(c, d):
        total = jnp.dot(s_all[0, crow(c), :], l_dense[d, 0:256, :], preferred_element_type=F32)
        for k in range(1, NX):
            total += jnp.dot(s_all[k, crow(c), :], l_dense[d, k * 256:(k + 1) * 256, :],
                             preferred_element_type=F32)
        return total

    def z_rows(h, c):
        size = CH // 2 if h == 0 else CH
        return pl.ds(pl.multiple_of(c * size, size), size)

    def z_copy(way, h, c):
        rows = z_rows(h, c)
        return remote(zs.at[way, h, rows], zr.at[way, h, rows], z_s.at[way, h, c], z_r.at[way, h, c],
                      at_z(1 if way == 0 else NZ - 1))

    def z_step(h, c):
        if h == 0:
            x_sum(c, 1 - p).wait_recv()
            x_sum_hop(c).wait_recv()
            total = product(c, 4)
            for way in range(2):
                zs[way, 0, z_rows(0, c), :] = total[way * (CH // 2):(way + 1) * (CH // 2)].astype(BF16)
                z_copy(way, 0, c).start()
            return
        for way in range(2):
            total = product(c, 4 - h if way == 0 else 4 + h)
            z_copy(way, h - 1, c).wait_recv()
            got = zr[way, h - 1, z_rows(h - 1, c), :].astype(F32)
            if h == 1:
                cut = CH // 2
                lo = pl.ds(c * CH, cut)
                hi = pl.ds(c * CH + cut, cut)
                if way == 0:
                    zs[way, h, lo, :] = (total[:cut] + got).astype(BF16)
                    zs[way, h, hi, :] = total[cut:].astype(BF16)
                else:
                    zs[way, h, lo, :] = total[:cut].astype(BF16)
                    zs[way, h, hi, :] = (total[cut:] + got).astype(BF16)
            else:
                zs[way, h, crow(c), :] = (total + got).astype(BF16)
            z_copy(way, h, c).start()

    def pair_out(c):
        rows = pl.ds(pl.multiple_of(p * HALF + c * CH, CH), CH)
        return remote(out.at[0, rows], out.at[0, rows], po_s.at[c], po_r.at[c], mate)

    pair_hole = remote(
        acc.at[pl.ds(pl.multiple_of((1 - p) * HALF, HALF), HALF)], hx, ph_s, ph_r, mate)

    def meta_send():
        get_code_once()
        lax.fori_loop(0, NT, sort_meta, 0, unroll=4)
        x_meta_two().start()
        x_meta(0).start()
        x_meta(1).start()

    def meta_wait():
        x_meta_two().wait_recv()
        x_meta(0).wait_recv()
        x_meta(1).wait_recv()

    def amp_send(j):
        y_amp(j, 0).start()
        y_amp(j, 1).start()

    def amp_pass(j):
        y_amp(j, p).wait_recv()
        y_hop(j).start()

    def block_send(d):
        get_code_once()
        sort_blocks(d)
        send_blocks(d)

    def block_build(d):
        if "meta" not in ready:
            ready.add("meta")
            meta_wait()
        build_blocks(d)

    def hole_part(k):
        if "h" not in ready:
            ready.add("h")
            for g in get_h:
                g.wait()
        if k == 0:
            hole(0, amp_v, "acc" not in ready)
        elif k == 1:
            hole(3 - 2 * p, a_all.at[2 - 2 * p], "acc" not in ready)
        elif k == 2:
            for j in range(NP):
                y_amp(j, 1 - p).wait_recv()
            hole(1 + 2 * p, a_all.at[2 * p], "acc" not in ready)
        else:
            for j in range(NP):
                y_hop(j).wait_recv()
            hole(2, a_all.at[1], "acc" not in ready)
        ready.add("acc")

    def own():
        for c in range(NC):
            fin[crow(c), :] = product(c, 0)

    def finish(c):
        if "hx" not in ready:
            ready.add("hx")
            pair_hole.wait_recv()
        z_copy(0, 3, c).wait_recv()
        z_copy(1, 3, c).wait_recv()
        rows = pl.ds(pl.multiple_of(p * HALF + c * CH, CH), CH)
        total = fin[crow(c), :] + acc[rows, :] + hx[crow(c), :]
        total += zr[0, 3, crow(c), :].astype(F32) + zr[1, 3, crow(c), :].astype(F32)
        out[0, rows, :] = total.astype(BF16)
        pair_out(c).start()

    ready = set()

    def get_code_once():
        if "code" not in ready:
            ready.add("code")
            get_code.wait()
            get_lraw.wait()

    steps = {
        "META": meta_send, "YS": amp_send, "YP": amp_pass, "LS": block_send, "LH": hop_blocks,
        "LX": share_x, "LY": share_y, "LZ": share_pass, "LP": swap_blocks, "LB": block_build, "SS": send_sum, "SH": hop_sum, "Z": z_step,
        "HO": hole_part, "PH": pair_hole.start, "OP": own, "FIN": finish,
    }
    for c in range(NC):
        pair_amp(c).start()
    for g in get_h:
        g.start()
    get_amp.wait()
    for step in PLAN:
        steps[step[0]](*step[1:])

    pair_hole.wait_send()
    for i in range(2):
        x_meta(i).wait_send()
    for j in range(NP):
        y_amp(j, 0).wait_send()
        y_amp(j, 1).wait_send()
        y_hop(j).wait_send()
    x_meta_two().wait_send()

    for d in range(NZ):
        pair_block(d).wait_send()
        if d in SHARED:
            for dx in (1, 2, 3):
                x_share(d, dx).wait_send()
            y_share(d, 0).wait_send()
            y_share(d, 1).wait_send()
            y_share_hop(d).wait_send()
            continue
        x_block(d, 0).wait_send()
        x_block(d, 1).wait_send()
        if d not in DIRECT:
            x_via(d).wait_send()
        x_hop(d).wait_send()

    def drain_c(c, carry):
        pair_amp(c).wait_send()
        x_sum(c, 0).wait_send()
        x_sum(c, 1).wait_send()
        x_sum_hop(c).wait_send()
        for way in range(2):
            for h in range(4):
                z_copy(way, h, c).wait_send()
        pair_out(c).wait_send()
        other = pl.ds(pl.multiple_of((1 - p) * HALF + c * CH, CH), CH)
        remote(out.at[0, other], out.at[0, other], po_s.at[c], po_r.at[c], mate).wait_recv()
        return carry

    lax.fori_loop(0, NC, drain_c, 0)


def on_device(amplitudes, hh_integrals, ladder_blocks, block_target, block_live):
    dma = pltpu.SemaphoreType.DMA
    any_space = pl.BlockSpec(memory_space=pl.ANY)
    vmem = pl.BlockSpec(memory_space=pltpu.VMEM)
    return pl.pallas_call(
        kernel,
        out_shape=pltpu.VMEM((1, ROWS, COLS), BF16),
        in_specs=[any_space] * 5,
        out_specs=vmem,
        scratch_shapes=[
            pltpu.VMEM((ROWS, COLS), BF16),
            pltpu.VMEM((HALF, COLS), BF16),
            pltpu.VMEM((NX, HALF, COLS), BF16),
            pltpu.VMEM((NY - 1, ROWS, COLS), BF16),
            pltpu.VMEM((NY, ROWS, ROWS), BF16),
            pltpu.VMEM((NT, TILE, TILE), BF16),
            pltpu.VMEM((NZ, 2, NX, TILE, TILE), BF16),
            pltpu.VMEM((NZ, 2, NX - 1, TILE, TILE), BF16),
            pltpu.VMEM((NZ, TILE, TILE), BF16),
            pltpu.VMEM((NX, 4 * NZ, TILE), F32),
            pltpu.VMEM((NX - 1, 4 * NZ, TILE), F32),
            pltpu.VMEM((1, NT), jnp.int32),
            pltpu.VMEM((1, NT), jnp.int32),
            pltpu.VMEM((NT, TILE), jnp.int32),
            pltpu.SMEM((NT, TILE), jnp.int32),
            pltpu.VMEM((NZ, NX * COLS, COLS), BF16),
            pltpu.VMEM((2, 4, HALF, COLS), BF16),
            pltpu.VMEM((2, 4, HALF, COLS), BF16),
            pltpu.VMEM((ROWS, COLS), F32),
            pltpu.VMEM((HALF, COLS), F32),
            pltpu.VMEM((HALF, COLS), F32),
            dma, dma, dma, dma, dma, dma((NY,)),
            dma((NC,)), dma((NC,)),
            dma((NP, 3)), dma((NP, 3)),
            dma((NC, 3)), dma((NC, 3)),
            dma((NZ, 4)), dma((NZ, 4)),
            dma((NZ, 3)), dma((NZ, 3)),
            dma((3,)), dma((3,)),
            dma((NZ,)), dma((NZ,)),
            dma((2, 4, NC)), dma((2, 4, NC)),
            dma, dma,
            dma((NC,)), dma((NC,)),
        ],
        compiler_params=pltpu.CompilerParams(
            collective_id=0, has_side_effects=True, vmem_limit_bytes=56 * 2**20),
        cost_estimate=pl.CostEstimate(
            flops=4 * ROWS * 4096 * COLS, bytes_accessed=12 * 2**20, transcendentals=0),
        name="ladder_hole",
    )(block_target, block_live, amplitudes, hh_integrals, ladder_blocks)


def solution(mesh):
    return jax.shard_map(
        on_device,
        mesh=mesh,
        in_specs=(
            P("pair", "occ", "vir"),
            P("pair", "occ", None),
            P("vir", None, None, None),
            P("vir", None),
            P("vir", None),
        ),
        out_specs=P("pair", "occ", "vir"),
        check_vma=False,
    )
```

time: 62.6 us -> 50.9 us (0.81)
  Pallas kernels: 59.3 us -> 50 us
  other arithmetic: 1.28 us -> 0 us
  local copies, waits for them, and re-layouts: 1.87 us -> 0.8 us
    pallas_call x1, Pallas kernels: 59.3 us -> 50 us  [on_device(): pl.pallas_call(kernel, out_shape=pltpu.VMEM((1, ROWS, COLS), BF16), in_sp...]
    reduce_sum x1 -> x0, other arithmetic: 1.28 us -> none  [on_device(): inverse = jnp.sum(jnp.where(hit, index[None, :], 0), axis=1)]
    unnamed x1, local copies, waits for them, and re-layouts: 1.87 us -> 0.8 us
where the time goes in v2:
time: 50.9 us; the launch traced here: 50.8 us
  Pallas kernels  50 us (98%)
  local copies, waits for them, and re-layouts  0.8 us (2%)
    pallas_call x1, Pallas kernels, on_device(): pl.pallas_call(kernel, out_shape=pltpu.VMEM((1, ROWS, COLS), BF16), in_sp...  50 us

profile of v2, /device:TPU:1, one launch (start us, length us, event | category | flops | bytes accessed | tf_op | source)
XLA Modules:
  0.0 50.8 jit_solution(5718039776114990391)
XLA Ops:
  0.0 50.0 %ladder_hole.1 = bf16[1,1024,256]{2,1,0:T(8,128)(2,1)S(1)} custom-call(s32[1,64]{1,0:T(1,128)} %target.1, s32[1,64]{1,0:T(1,128)} %live.1, bf16[1,1024,256]{2,1,0:T(8,128)(2,1)} %amp.1, bf16[1,1024,4096]{2,1,0:T(8,128)(2,1)} %hh.1, bf16[1,64,128,128]{3,2,1,0:T(8,128)(2,1)} %blocks.1), custom_call_target="tpu_custom_call" | custom-call | flops 4294967296 | bytes 12582912 | tf_op jit(solution)/shard_map/ladder_hole/pallas_call | solution.py:454
  50.0 0.8 %copy.7 = bf16[1,1024,256]{2,1,0:T(8,128)(2,1)} copy(bf16[1,1024,256]{2,1,0:T(8,128)(2,1)S(1)} %ladder_hole.1) | data formatting | bytes 1048576

commit v3 on v2

--- a/solution.py
+++ b/solution.py
@@ -18,19 +18,19 @@
 NC = HALF // CH
 NP = 4
 PIECE = ROWS // NP
-DIRECT = (4,)
-SHARED = (3, 5)
+DIRECT = ()
+SHARED = (4, 3, 5)
 
 PLAN = (
-    ("LX", 3), ("LX", 5), ("LS", 4), ("SS", 1), ("LY", 5), ("SS", 3), ("LY", 3), ("SS", 0), ("META",),
-    ("LZ", 5), ("LZ", 3), ("LP", 4), ("SH", 1), ("YS", 1), ("SH", 3), ("LS", 6), ("LP", 3), ("SH", 0),
-    ("SS", 2), ("LB", 4), ("LS", 2), ("Z", 0, 3), ("LP", 5), ("LS", 0), ("YS", 3), ("LH", 6), ("Z", 0, 0),
-    ("Z", 0, 1), ("SH", 2), ("LB", 3), ("LB", 5), ("Z", 1, 3), ("YS", 2), ("LH", 2), ("YS", 0), ("LS", 7),
-    ("Z", 1, 0), ("LH", 0), ("LP", 6), ("YP", 1), ("LS", 1), ("Z", 0, 2), ("LP", 2), ("Z", 1, 1), ("LH", 7),
-    ("LP", 0), ("LB", 6), ("LB", 2), ("Z", 2, 3), ("LH", 1), ("Z", 1, 2), ("YP", 3), ("Z", 2, 0), ("LP", 7),
-    ("HO", 0), ("YP", 0), ("Z", 2, 1), ("LP", 1), ("HO", 2), ("LB", 0), ("OP",), ("YP", 2), ("Z", 2, 2),
-    ("LB", 7), ("HO", 1), ("LB", 1), ("Z", 3, 0), ("Z", 3, 3), ("Z", 3, 2), ("HO", 3), ("Z", 3, 1), ("PH",),
-    ("FIN", 2), ("FIN", 3), ("FIN", 0), ("FIN", 1),
+    ("YS", 1), ("LX", 4), ("LX", 5), ("LX", 3), ("SS", 3), ("SS", 0), ("LY", 4), ("LY", 5), ("LY", 3),
+    ("SS", 2), ("SS", 1), ("META",), ("LZ", 4), ("LZ", 5), ("SH", 3), ("HO", 0), ("SH", 0), ("LZ", 3),
+    ("SH", 2), ("YS", 0), ("LP", 4), ("LP", 5), ("SH", 1), ("LB", 4), ("LS", 6), ("YP", 1), ("YS", 2),
+    ("LS", 2), ("Z", 0, 3), ("Z", 0, 0), ("LP", 3), ("Z", 0, 2), ("LS", 7), ("YS", 3), ("Z", 0, 1),
+    ("LB", 3), ("LH", 6), ("LB", 5), ("Z", 1, 3), ("LH", 2), ("Z", 1, 2), ("LS", 1), ("Z", 1, 0), ("YP", 0),
+    ("LH", 7), ("LP", 6), ("Z", 1, 1), ("LP", 2), ("LH", 1), ("LB", 6), ("LB", 2), ("YP", 2), ("Z", 2, 3),
+    ("Z", 2, 2), ("LS", 0), ("LP", 7), ("Z", 2, 0), ("YP", 3), ("LB", 7), ("HO", 2), ("HO", 1), ("LH", 0),
+    ("LP", 1), ("Z", 2, 1), ("LB", 1), ("Z", 3, 3), ("LP", 0), ("Z", 3, 0), ("LB", 0), ("Z", 3, 2), ("OP",),
+    ("Z", 3, 1), ("HO", 3), ("PH",), ("FIN", 2), ("FIN", 0), ("FIN", 3), ("FIN", 1),
 )
 F32 = jnp.float32
 BF16 = jnp.bfloat16

time: 50.9 us -> 49.8 us (0.978)
  Pallas kernels: 50 us -> 48.9 us
    pallas_call x1, Pallas kernels: 50 us -> 48.9 us  [on_device(): pl.pallas_call(kernel, out_shape=pltpu.VMEM((1, ROWS, COLS), BF16), in_sp...]
where the time goes in v3:
time: 49.8 us
  Pallas kernels  48.9 us (98%)
  local copies, waits for them, and re-layouts  0.8 us (2%)
    pallas_call x1, Pallas kernels, on_device(): pl.pallas_call(kernel, out_shape=pltpu.VMEM((1, ROWS, COLS), BF16), in_sp...  48.9 us

profile of v3, /device:TPU:1, one launch (start us, length us, event | category | flops | bytes accessed | tf_op | source)
XLA Modules:
  0.0 49.8 jit_solution(10165774831651570902)
XLA Ops:
  0.0 48.9 %ladder_hole.1 = bf16[1,1024,256]{2,1,0:T(8,128)(2,1)S(1)} custom-call(s32[1,64]{1,0:T(1,128)} %target.1, s32[1,64]{1,0:T(1,128)} %live.1, bf16[1,1024,256]{2,1,0:T(8,128)(2,1)} %amp.1, bf16[1,1024,4096]{2,1,0:T(8,128)(2,1)} %hh.1, bf16[1,64,128,128]{3,2,1,0:T(8,128)(2,1)} %blocks.1), custom_call_target="tpu_custom_call" | custom-call | flops 4294967296 | bytes 12582912 | tf_op jit(solution)/shard_map/ladder_hole/pallas_call | solution.py:454
  49.0 0.8 %copy.7 = bf16[1,1024,256]{2,1,0:T(8,128)(2,1)} copy(bf16[1,1024,256]{2,1,0:T(8,128)(2,1)S(1)} %ladder_hole.1) | data formatting | bytes 1048576

commit v4 on v3

--- a/solution.py
+++ b/solution.py
@@ -22,15 +22,15 @@
 SHARED = (4, 3, 5)
 
 PLAN = (
-    ("YS", 1), ("LX", 4), ("LX", 5), ("LX", 3), ("SS", 3), ("SS", 0), ("LY", 4), ("LY", 5), ("LY", 3),
-    ("SS", 2), ("SS", 1), ("META",), ("LZ", 4), ("LZ", 5), ("SH", 3), ("HO", 0), ("SH", 0), ("LZ", 3),
-    ("SH", 2), ("YS", 0), ("LP", 4), ("LP", 5), ("SH", 1), ("LB", 4), ("LS", 6), ("YP", 1), ("YS", 2),
-    ("LS", 2), ("Z", 0, 3), ("Z", 0, 0), ("LP", 3), ("Z", 0, 2), ("LS", 7), ("YS", 3), ("Z", 0, 1),
-    ("LB", 3), ("LH", 6), ("LB", 5), ("Z", 1, 3), ("LH", 2), ("Z", 1, 2), ("LS", 1), ("Z", 1, 0), ("YP", 0),
-    ("LH", 7), ("LP", 6), ("Z", 1, 1), ("LP", 2), ("LH", 1), ("LB", 6), ("LB", 2), ("YP", 2), ("Z", 2, 3),
-    ("Z", 2, 2), ("LS", 0), ("LP", 7), ("Z", 2, 0), ("YP", 3), ("LB", 7), ("HO", 2), ("HO", 1), ("LH", 0),
-    ("LP", 1), ("Z", 2, 1), ("LB", 1), ("Z", 3, 3), ("LP", 0), ("Z", 3, 0), ("LB", 0), ("Z", 3, 2), ("OP",),
-    ("Z", 3, 1), ("HO", 3), ("PH",), ("FIN", 2), ("FIN", 0), ("FIN", 3), ("FIN", 1),
+    ("LX", 4), ("LX", 3), ("YS", 3), ("LX", 5), ("SS", 0), ("LY", 4), ("SS", 3), ("LY", 3), ("SS", 1),
+    ("SS", 2), ("LY", 5), ("META",), ("LZ", 4), ("LZ", 3), ("LZ", 5), ("SH", 0), ("YS", 2), ("SH", 1),
+    ("LP", 4), ("SH", 3), ("LP", 3), ("SH", 2), ("LP", 5), ("LS", 2), ("LB", 4), ("Z", 0, 0), ("LS", 6),
+    ("YS", 1), ("LS", 1), ("Z", 0, 1), ("YS", 0), ("Z", 0, 3), ("Z", 0, 2), ("LB", 5), ("LB", 3), ("YP", 2),
+    ("Z", 1, 0), ("LH", 6), ("YP", 3), ("LH", 2), ("LS", 7), ("Z", 1, 3), ("Z", 1, 2), ("LH", 1),
+    ("Z", 1, 1), ("LP", 6), ("LP", 2), ("LH", 7), ("YP", 1), ("LS", 0), ("LB", 6), ("LP", 1), ("YP", 0),
+    ("LB", 2), ("Z", 2, 0), ("LP", 7), ("Z", 2, 2), ("LH", 0), ("Z", 2, 3), ("Z", 2, 1), ("LB", 1),
+    ("LP", 0), ("LB", 7), ("Z", 3, 2), ("LB", 0), ("Z", 3, 0), ("HO", 3), ("HO", 2), ("OP",), ("Z", 3, 1),
+    ("HO", 1), ("HO", 0), ("Z", 3, 3), ("PH",), ("FIN", 1), ("FIN", 2), ("FIN", 0), ("FIN", 3),
 )
 F32 = jnp.float32
 BF16 = jnp.bfloat16

time: 49.8 us -> 53 us (1.064)
  Pallas kernels: 48.9 us -> 52.1 us
    pallas_call x1, Pallas kernels: 48.9 us -> 52.1 us  [on_device(): pl.pallas_call(kernel, out_shape=pltpu.VMEM((1, ROWS, COLS), BF16), in_sp...]
where the time goes in v4:
time: 53 us; the launch traced here: 52.9 us
  Pallas kernels  52.1 us (98%)
  local copies, waits for them, and re-layouts  0.8 us (2%)
    pallas_call x1, Pallas kernels, on_device(): pl.pallas_call(kernel, out_shape=pltpu.VMEM((1, ROWS, COLS), BF16), in_sp...  52.1 us

profile of v4, /device:TPU:1, one launch (start us, length us, event | category | flops | bytes accessed | tf_op | source)
XLA Modules:
  0.0 52.9 jit_solution(6898199790156677290)
XLA Ops:
  0.0 52.1 %ladder_hole.1 = bf16[1,1024,256]{2,1,0:T(8,128)(2,1)S(1)} custom-call(s32[1,64]{1,0:T(1,128)} %target.1, s32[1,64]{1,0:T(1,128)} %live.1, bf16[1,1024,256]{2,1,0:T(8,128)(2,1)} %amp.1, bf16[1,1024,4096]{2,1,0:T(8,128)(2,1)} %hh.1, bf16[1,64,128,128]{3,2,1,0:T(8,128)(2,1)} %blocks.1), custom_call_target="tpu_custom_call" | custom-call | flops 4294967296 | bytes 12582912 | tf_op jit(solution)/shard_map/ladder_hole/pallas_call | solution.py:454
  52.1 0.8 %copy.7 = bf16[1,1024,256]{2,1,0:T(8,128)(2,1)} copy(bf16[1,1024,256]{2,1,0:T(8,128)(2,1)S(1)} %ladder_hole.1) | data formatting | bytes 1048576
